TPU v7x, 32 devices: a whole 2x2x4 slice. The times are simulated.
32 devices in a mesh: seq: 8 (over z, x), tensor: 4 (over y, core).
Axes of the slice: x: 2, y: 2, z: 4, core: 2. Of those that a mesh axis runs over, the one named last changes fastest.
Arguments:
- queries: bfloat16 [7168, 2048], P('seq', 'tensor'), may hold values from -256 to 256
- db_states: bfloat16 [128, 64, 896], P('seq', None, 'tensor'), may hold values from -4096 to 4096
- enc_gain: float32 [896], replicated, may hold values from 0.1 to 1.9
- kv_weight: bfloat16 [896, 2, 2048], P(None, None, 'tensor'), may hold values from -0.1875 to 0.1875
- shard_ids: int32 [112, 2], P('seq'), may hold values from 0 to 7, as said below
- offsets: int32 [112, 2], P('seq'), may hold values from 0 to 14
Outputs:
- attention_out: bfloat16 [7168, 2048], P('seq', 'tensor')
Inputs may be any that keep to these rules, and one draw needn't show every extreme that they name: `shard_ids`: the neighbours named by the 14 groups of one device lie at most 4 in any one shard, and some shard is named exactly 4 times by the groups of every device.
All inputs are finite; a program needn't handle non-finite values.
Results may differ from a plain program's by a relative error of at most 0.0087.
Values may be sent and summed in bfloat16 or wider, within the bound.
A program may use at most 64 MiB of HBM per device.

v0:
```python
import math
import jax
import jax.numpy as jnp
from jax import lax
from jax.sharding import PartitionSpec as P

HEAD_DIM = 128
epsilon = 1e-06


def passed_along(block, axis, distance):
    devices = range(lax.axis_size(axis))
    route = [(i - distance, i) for i in devices if i - distance in devices]
    return lax.ppermute(block, axis, route)


def attend(query_win, kv_win):
    scores = jnp.einsum(
        "wqhd,wkhd->whqk", query_win, kv_win[:, :, 0], preferred_element_type=jnp.float32
    ) / math.sqrt(HEAD_DIM)
    highest = jnp.max(scores, axis=-1, keepdims=True)
    expo = jnp.exp(scores - highest)
    weights = (expo / jnp.sum(expo, axis=-1, keepdims=True)).astype(jnp.bfloat16)
    mixed = jnp.einsum(
        "whqk,wkhd->wqhd", weights, kv_win[:, :, 1], preferred_element_type=jnp.float32
    ).astype(jnp.bfloat16)
    return mixed.reshape(query_win.shape[0] * query_win.shape[1], -1)


def per_device(queries, db_states, enc_gain, kv_weight, shard_ids, offsets):
    seq_count = lax.axis_size("seq")
    group_count = shard_ids.shape[0]
    neigh_count = 2 * group_count
    slot_cap = (neigh_count + seq_count - 1) // seq_count
    group_len = db_states.shape[1]
    enc_width = kv_weight.shape[0]
    head_count = kv_weight.shape[2] // HEAD_DIM
    tok_count = queries.shape[0]
    query_cols = queries.shape[1]
    projection = kv_weight.reshape(enc_width, -1)
    token_rows = neigh_count * 2 * group_len
    neigh_shard = shard_ids.reshape(neigh_count)
    neigh_offset = offsets.reshape(neigh_count)
    owners = jnp.arange(seq_count, dtype=jnp.int32)
    onehot = (neigh_shard[:, None] == owners[None, :]).astype(jnp.int32)
    before = jnp.cumsum(onehot, axis=0) - onehot
    order_rank = jnp.sum(before * onehot, axis=1)
    slot_index = neigh_shard * slot_cap + order_rank
    table = jnp.zeros((seq_count * slot_cap,), jnp.int32).at[slot_index].set(neigh_offset + 1)
    wanted = lax.all_to_all(
        table.reshape(seq_count, slot_cap), "seq", split_axis=0, concat_axis=0, tiled=True
    )
    first_group = jnp.maximum(wanted - 1, 0)
    stored = db_states.reshape(db_states.shape[0], -1)
    outgoing = jnp.stack(
        [jnp.take(stored, first_group, axis=0), jnp.take(stored, first_group + 1, axis=0)], axis=2
    )
    incoming = lax.all_to_all(outgoing, "seq", split_axis=0, concat_axis=0, tiled=True)
    picked = jnp.take(incoming.reshape(seq_count * slot_cap, 2, -1), slot_index, axis=0)
    enc_rows = picked.reshape(token_rows, -1)
    as_float = lax.all_gather(enc_rows, "tensor", axis=1, tiled=True).astype(jnp.float32)
    scaled = (as_float * enc_gain[None, :]).astype(jnp.bfloat16)
    kv_sum = jnp.dot(scaled, projection, preferred_element_type=jnp.float32)
    kv_sum, square_sum = (kv_sum, jnp.sum(as_float * as_float, axis=1))
    inv_rms = lax.rsqrt(square_sum / enc_width + epsilon)
    keys_values = (kv_sum * inv_rms[:, None]).astype(jnp.bfloat16)
    kv_groups = keys_values.reshape(group_count, 4 * group_len, 2, head_count, HEAD_DIM)
    previous = passed_along(kv_groups[group_count - 1], "seq", 1)
    padded = jnp.concatenate(
        [
            jnp.zeros((1, query_cols), jnp.bfloat16),
            queries,
            jnp.zeros((group_len - 1, query_cols), jnp.bfloat16),
        ],
        axis=0,
    )
    windows = padded.reshape(group_count + 1, group_len, head_count, HEAD_DIM)
    attended = attend(windows, jnp.concatenate([previous[None], kv_groups], axis=0))
    result = attended[1 : tok_count + 1]
    return result


def solution(mesh):
    return jax.shard_map(
        per_device,
        mesh=mesh,
        in_specs=(
            P("seq", "tensor"),
            P("seq", None, "tensor"),
            P(),
            P(None, None, "tensor"),
            P("seq", None),
            P("seq", None),
        ),
        out_specs=P("seq", "tensor"),
        check_vma=False,
    )
```

profile of v0, /device:TPU:0, one launch (start us, length us, event | category | flops | bytes accessed | tf_op | source)
XLA Modules:
  0.0 213.9 jit_solution(16390059754301208129)
XLA Ops:
  6.5 0.7 broadcast_multiply_fusion
  7.2 0.8 copy.47
  8.0 0.7 broadcast_add_fusion
  10.8 7.3 %all-to-all-start = ((s32[8,1,4]{2,1,0:T(1,128)}), s32[8,1,4]{2,1,0:T(1,128)S(1)}, u32[]{:S(2)}, u32[]{:S(2)}) async-start(s32[8,1,4]{2,1,0:T(1,128)} %bitcast.2), calls=%async_computation | async-start | bytes 8192 | tf_op jit(solution)/shard_map/all_to_all | solution.py:50
  18.0 1.9 reshape.89
  20.0 4.5 %all-to-all-done = s32[8,1,4]{2,1,0:T(1,128)S(1)} async-done(((s32[8,1,4]{2,1,0:T(1,128)}), s32[8,1,4]{2,1,0:T(1,128)S(1)}, u32[]{:S(2)}, u32[]{:S(2)}) %all-to-all-start) | async-done | bytes 160 | tf_op jit(solution)/shard_map/all_to_all | solution.py:50
  25.1 1.1 gather_fusion.2
  26.5 1.1 gather_fusion.1
  28.0 0.9 select_bitcast_fusion
  28.9 2.5 %pad_maximum_fusion.1 = bf16[8,4,2,14336]{3,1,2,0:T(4,128)(2,1)} fusion(bf16[8,4,1,14336]{3,1,2,0:T(4,128)(2,1)S(1)} %get-tuple-element.10, bf16[8,4,1,14336]{3,1,2,0:T(4,128)(2,1)S(1)} %get-tuple-element.11), kind=kLoop, calls=%fused_computation.27 | loop fusion | flops 917504 | bytes 3670016 | tf_op jit(solution)/shard_map/stack | solution.py:55
  31.4 3.6 %all-to-all-start.1 = ((bf16[8,4,2,14336]{3,1,2,0:T(4,128)(2,1)}), bf16[8,4,2,14336]{3,1,2,0:T(4,128)(2,1)S(1)}, u32[]{:S(2)}, u32[]{:S(2)}) async-start(bf16[8,4,2,14336]{3,1,2,0:T(4,128)(2,1)} %pad_maximum_fusion.1), calls=%async_computation.1 | async-start | bytes 3670016 | tf_op jit(solution)/shard_map/all_to_all | solution.py:58
  35.3 41.1 %all-to-all-done.1 = bf16[8,4,2,14336]{3,1,2,0:T(4,128)(2,1)S(1)} async-done(((bf16[8,4,2,14336]{3,1,2,0:T(4,128)(2,1)}), bf16[8,4,2,14336]{3,1,2,0:T(4,128)(2,1)S(1)}, u32[]{:S(2)}, u32[]{:S(2)}) %all-to-all-start.1) | async-done | bytes 1835040 | tf_op jit(solution)/shard_map/all_to_all | solution.py:58
  76.4 3.1 %copy.56 = bf16[8,4,2,14336]{3,2,1,0:T(2,128)(2,1)} copy(bf16[8,4,2,14336]{3,1,2,0:T(4,128)(2,1)S(1)} %all-to-all-done.1) | data formatting | bytes 3670016 | tf_op jit(solution)/shard_map/all_to_all | solution.py:58
  79.5 5.3 %gather_fusion = bf16[28,2,14336]{2,1,0:T(2,128)(2,1)S(1)} fusion(bf16[32,2,14336]{2,1,0:T(2,128)(2,1)} %bitcast.48, s32[1024]{0:T(1024)S(1)} %pad_clamp_fusion), kind=kCustom, calls=%fused_computation.2 | custom fusion | bytes 3211376 | tf_op jit(solution)/shard_map/jit(_take)/gather | solution.py:59
  84.8 1.5 broadcast_select_fusion
  86.3 2.6 %select_n.35 = bf16[3584,224]{1,0:T(8,128)(2,1)S(1)} reshape(bf16[28,2,14336]{2,1,0:T(2,128)(2,1)S(1)} %broadcast_select_fusion) | data formatting | bytes 3211264 | tf_op jit(solution)/shard_map/jit(_take)/select_n | solution.py:59
  89.0 2.6 %copy.57 = bf16[3584,224]{0,1:T(8,128)(2,1)} copy(bf16[3584,224]{1,0:T(8,128)(2,1)S(1)} %select_n.35) | data formatting | bytes 3211264 | tf_op jit(solution)/shard_map/jit(_take)/select_n | solution.py:59
  91.6 2.0 copy.65
  93.6 44.3 %all-gather.2.cloned.1.call-done = bf16[3584,896]{0,1:T(8,128)(2,1)} async-done(((bf16[3584,224]{0,1:T(8,128)(2,1)}), bf16[3584,896]{0,1:T(8,128)(2,1)}) %all-gather.2.cloned.1.call-update) | async-done | bytes 6422544 | tf_op jit(solution)/shard_map/all_gather | solution.py:61
  137.9 4.3 %fusion.2 = f32[3584]{0:T(1024)S(1)} fusion(bf16[3584,896]{0,1:T(8,128)(2,1)} %all-gather.2.cloned.1.call-done), kind=kLoop, calls=%fused_computation.9 | loop fusion | flops 9630208 | bytes 6436864 | tf_op jit(solution)/shard_map/reduce_sum | solution.py:64
  142.5 8.7 %multiply_convert_fusion = bf16[3584,1024]{0,1:T(8,128)(2,1)S(1)} fusion(bf16[896,1024]{1,0:T(8,128)(2,1)S(1)} %bitcast.53, f32[3584]{0:T(1024)S(1)} %add_rsqrt_fusion, bf16[3584,896]{0,1:T(8,128)(2,1)S(1)} %copy-done.1, f32[896]{0:T(1024)S(1)} %copy-done.4), kind=kOutput, calls=%fused_computation.7 | convolution fusion | flops 6593642496 | bytes 15615488 | tf_op jit(solution)/shard_map/dot_general | solution.py:63
  151.2 3.0 %copy-done = bf16[3584,1024]{0,1:T(8,128)(2,1)} copy-done((bf16[3584,1024]{0,1:T(8,128)(2,1)}, bf16[3584,1024]{0,1:T(8,128)(2,1)S(1)}, u32[]{:S(2)}) %copy-start) | copy-done | bytes 7340056
  154.2 1.0 copy.58
  155.2 3.4 %collective-permute-start = (bf16[256,2,4,128]{3,0,2,1:T(8,128)(2,1)}, bf16[256,2,4,128]{3,0,2,1:T(8,128)(2,1)S(1)}, u32[]{:S(2)}, u32[]{:S(2)}) collective-permute-start(bf16[256,2,4,128]{3,0,2,1:T(8,128)(2,1)} %copy.58), channel_id=1, source_target_pairs={{0,4},{4,8},{8,12},{12,16},{16,20},{20,24},{24,28},{1,5},{5,9},{9,... | collective-permute-start | bytes 1572872 | tf_op jit(solution)/shard_map/ppermute | solution.py:14
  159.4 13.7 %reshape.139 = bf16[14,256,2,4,128]{1,0,4,3,2:T(8,128)(2,1)} reshape(bf16[3584,1024]{0,1:T(8,128)(2,1)} %copy-done) | data formatting | bytes 14680064 | tf_op jit(solution)/shard_map/reshape | solution.py:67
  173.1 14.2 %copy.60 = bf16[14,256,2,4,128]{4,1,3,0,2:T(8,128)(2,1)} copy(bf16[14,256,2,4,128]{1,0,4,3,2:T(8,128)(2,1)} %reshape.139) | data formatting | bytes 14680064 | tf_op jit(solution)/shard_map/reshape | solution.py:67
  187.3 3.1 %fusion.7 = f32[15,4,64,256]{3,2,1,0:T(8,128)S(1)} fusion(bf16[1,256,2,4,128]{4,1,3,0,2:T(8,128)(2,1)S(1)} %bitcast.54, bf16[14,256,2,4,128]{4,1,3,0,2:T(8,128)(2,1)} %copy.60, bf16[15,64,4,128]{3,2,1,0:T(4,128)(2,1)S(1)} %reshape.93), kind=kOutput, calls=%fused_computation.15 | convolution fusion | flops 253624320 | bytes 12779520 | tf_op jit(solution)/shard_map/wqhd,wkhd->whqk/dot_general | solution.py:18
  190.4 1.9 copy-done.2
  192.3 1.5 fusion.39
  193.7 11.2 %fusion.21 = bf16[15,64,4,128]{3,1,2,0:T(8,128)(2,1)S(1)} fusion(bf16[14,256,2,4,128]{4,1,3,0,2:T(8,128)(2,1)} %copy.60, bf16[1,256,2,4,128]{4,1,3,0,2:T(8,128)(2,1)S(1)} %bitcast.55, f32[15,4,64]{2,1,0:T(4,128)S(1)} %fusion.39, f32[15,4,64,256]{3,2,1,0:T(8,128)} %copy-done.2), kind=kOutput, calls=%fused_computation.29 | convolution fusion | flops 264933376 | bytes 12794880 | tf_op jit(solution)/shard_map/whqk,wkhd->wqhd/dot_general | solution.py:24
  204.9 0.8 copy.62
  205.9 1.1 slice.26
  (45 shorter events, 5.0 us)
Async XLA Ops:
  10.8 13.6 %all-to-all-start = ((s32[8,1,4]{2,1,0:T(1,128)}), s32[8,1,4]{2,1,0:T(1,128)S(1)}, u32[]{:S(2)}, u32[]{:S(2)}) async-start(s32[8,1,4]{2,1,0:T(1,128)} %bitcast.2), calls=%async_computation | async-start | bytes 8192 | tf_op jit(solution)/shard_map/all_to_all | solution.py:50
  31.4 45.0 %all-to-all-start.1 = ((bf16[8,4,2,14336]{3,1,2,0:T(4,128)(2,1)}), bf16[8,4,2,14336]{3,1,2,0:T(4,128)(2,1)S(1)}, u32[]{:S(2)}, u32[]{:S(2)}) async-start(bf16[8,4,2,14336]{3,1,2,0:T(4,128)(2,1)} %pad_maximum_fusion.1), calls=%async_computation.1 | async-start | bytes 3670016 | tf_op jit(solution)/shard_map/all_to_all | solution.py:58
  35.0 102.9 %all-gather.2.cloned.1.call-start = ((), (), s32[]{:S(2)}) async-start(), calls=%async_computation.2 | async-start | bytes 8028160 | tf_op jit(solution)/shard_map/all_gather | solution.py:61
  93.6 48.6 %copy-start.4 = (f32[896]{0:T(1024)S(1)}, f32[896]{0:T(1024)}, u32[]{:S(2)}) copy-start(f32[896]{0:T(1024)} %param.10) | copy-start | bytes 10756
  137.9 4.7 %copy-start.1 = (bf16[3584,896]{0,1:T(8,128)(2,1)S(1)}, bf16[3584,896]{0,1:T(8,128)(2,1)}, u32[]{:S(2)}) copy-start(bf16[3584,896]{0,1:T(8,128)(2,1)} %all-gather.2.cloned.1.call-done) | copy-start | bytes 19267588
  142.5 16.2 %copy-start.3 = (bf16[896,512]{1,0:T(8,128)(2,1)S(1)}, bf16[896,512]{1,0:T(8,128)(2,1)}, u32[]{:S(2)}) copy-start(bf16[896,512]{1,0:T(8,128)(2,1)} %param.8) | copy-start | bytes 2752516
  151.2 3.0 %copy-start = (bf16[3584,1024]{0,1:T(8,128)(2,1)}, bf16[3584,1024]{0,1:T(8,128)(2,1)S(1)}, u32[]{:S(2)}) copy-start(bf16[3584,1024]{0,1:T(8,128)(2,1)S(1)} %multiply_convert_fusion) | copy-start | bytes 22020100
  155.2 32.0 %collective-permute-start = (bf16[256,2,4,128]{3,0,2,1:T(8,128)(2,1)}, bf16[256,2,4,128]{3,0,2,1:T(8,128)(2,1)S(1)}, u32[]{:S(2)}, u32[]{:S(2)}) collective-permute-start(bf16[256,2,4,128]{3,0,2,1:T(8,128)(2,1)} %copy.58), channel_id=1, source_target_pairs={{0,4},{4,8},{8,12},{12,16},{16,20},{20,24},{24,28},{1,5},{5,9},{9,... | collective-permute-start | bytes 1572872 | tf_op jit(solution)/shard_map/ppermute | solution.py:14
  190.4 1.9 copy-start.2
Sparse Core Ops, SparseCore 0:
  91.7 46.1 all-gather.1
where the time goes:
time: 215 us; the launch traced here: 214 us
  waiting for transfers between devices  89.9 us (42%)
  local copies, waits for them, and re-layouts  60.2 us (28%)
  matrix products  23 us (11%)
  starting transfers between devices  14.4 us (7%)
  between operations  13.6 us (6%)
  other arithmetic  12.7 us (6%)
    all_gather x1, waiting for transfers between devices, per_device(): lax.all_gather(enc_rows, 'tensor', axis=1, tiled=True).astype(jnp.float32)  44.3 us
    all_to_all x1, waiting for transfers between devices, per_device(): lax.all_to_all(outgoing, 'seq', split_axis=0, concat_axis=0, tiled=True)  41.1 us
    reshape x2, local copies, waits for them, and re-layouts, per_device(): keys_values.reshape(group_count, 4 * group_len, 2, head_count, HEAD_DIM)  27.9 us
    dot_general x1, matrix products, attend(): jnp.einsum('whqk,wkhd->wqhd', weights, kv_win[:, :, 1], preferred_element...  11.2 us
    dot_general x1, matrix products, per_device(): kv_sum = jnp.dot(scaled, projection, preferred_element_type=jnp.float32)  8.67 us
    unnamed x13, local copies, waits for them, and re-layouts  8.17 us
    all_to_all x1, starting transfers between devices, per_device(): lax.all_to_all(table.reshape(seq_count, slot_cap), 'seq', split_axis=0, c...  7.25 us
    gather x1, local copies, waits for them, and re-layouts, per_device(): jnp.take(incoming.reshape(seq_count * slot_cap, 2, -1), slot_index, axis=0)  5.28 us
  transfers between devices with their start and end apart: 4, of which 3 were waited for; matrix products, arithmetic and copies ran while one was open for 15% of the time, Pallas kernels for 0%

commit v1 on v0

--- a/solution.py
+++ b/solution.py
@@ -6,6 +6,25 @@
 
 HEAD_DIM = 128
 epsilon = 1e-06
+
+
+def collect(value, axis, dim):
+    size, index, rows = (lax.axis_size(axis), lax.axis_index(axis), value.shape[dim])
+    right = [(i, (i + 1) % size) for i in range(size)]
+    behind = [(i, (i - 1) % size) for i in range(size)]
+    out = jnp.zeros((*value.shape[:dim], size * rows, *value.shape[dim + 1 :]), value.dtype)
+    out = lax.dynamic_update_slice_in_dim(out, value, index * rows, axis=dim)
+    from_left = from_right = value
+    half = size // 2
+    for lap in range(1, half + 1):
+        from_left = lax.ppermute(from_left, axis, right)
+        out = lax.dynamic_update_slice_in_dim(out, from_left, (index - lap) % size * rows, axis=dim)
+        if lap < size - half:
+            from_right = lax.ppermute(from_right, axis, behind)
+            out = lax.dynamic_update_slice_in_dim(
+                out, from_right, (index + lap) % size * rows, axis=dim
+            )
+    return out
 
 
 def passed_along(block, axis, distance):
@@ -58,7 +77,7 @@
     incoming = lax.all_to_all(outgoing, "seq", split_axis=0, concat_axis=0, tiled=True)
     picked = jnp.take(incoming.reshape(seq_count * slot_cap, 2, -1), slot_index, axis=0)
     enc_rows = picked.reshape(token_rows, -1)
-    as_float = lax.all_gather(enc_rows, "tensor", axis=1, tiled=True).astype(jnp.float32)
+    as_float = collect(enc_rows, "tensor", 1).astype(jnp.float32)
     scaled = (as_float * enc_gain[None, :]).astype(jnp.bfloat16)
     kv_sum = jnp.dot(scaled, projection, preferred_element_type=jnp.float32)
     kv_sum, square_sum = (kv_sum, jnp.sum(as_float * as_float, axis=1))

time: 215 us -> 283 us (1.32); the launches traced: 214 us -> 278 us
  local copies, waits for them, and re-layouts: 60.2 us -> 144 us
  between operations: 13.6 us -> 0.25 us
  waiting for transfers between devices: 89.9 us -> 79.6 us
    dynamic_update_slice x0 -> x4, local copies, waits for them, and re-layouts: none -> 73.3 us  [the longest x2 37.3 us: collect(): lax.dynamic_update_slice_in_dim(out, from_left, (index - lap) % size * ro...]
    all_gather x1 -> x0, waiting for transfers between devices: 44.3 us -> none  [per_device(): lax.all_gather(enc_rows, 'tensor', axis=1, tiled=True).astype(jnp.float32)]
    ppermute x0 -> x3, waiting for transfers between devices: none -> 34 us  [the longest x2 34 us: collect(): from_left = lax.ppermute(from_left, axis, right)]
    ppermute x0 -> x3, local copies, waits for them, and re-layouts: none -> 7.08 us  [the longest x2 4.25 us: collect(): from_left = lax.ppermute(from_left, axis, right)]
    broadcast_in_dim x0 -> x1, local copies, waits for them, and re-layouts: none -> 3.17 us  [collect(): jnp.zeros((*value.shape[:dim], size * rows, *value.shape[dim + 1:]), valu...]
  transfers between devices with their start and end apart: 4 -> 6, of which waited for: 3 -> 3; matrix products, arithmetic and copies ran while one was open for 15% -> 34% of each run, Pallas kernels for 0% -> 0%
where the time goes in v1:
time: 283 us; the launch traced here: 278 us
  local copies, waits for them, and re-layouts  144 us (51%)
  waiting for transfers between devices  79.6 us (28%)
  matrix products  24.1 us (9%)
  starting transfers between devices  16.7 us (6%)
  other arithmetic  12.8 us (5%)
    all_to_all x1, waiting for transfers between devices, per_device(): lax.all_to_all(outgoing, 'seq', split_axis=0, concat_axis=0, tiled=True)  41.2 us
    dynamic_update_slice x2, local copies, waits for them, and re-layouts, collect(): lax.dynamic_update_slice_in_dim(out, from_left, (index - lap) % size * ro...  37.3 us
    ppermute x2, waiting for transfers between devices, collect(): from_left = lax.ppermute(from_left, axis, right)  34 us
    reshape x2, local copies, waits for them, and re-layouts, per_device(): keys_values.reshape(group_count, 4 * group_len, 2, head_count, HEAD_DIM)  27.6 us
    dynamic_update_slice x1, local copies, waits for them, and re-layouts, collect(): lax.dynamic_update_slice_in_dim(out, from_right, (index + lap) % size * r...  19 us
    dynamic_update_slice x1, local copies, waits for them, and re-layouts, collect(): out = lax.dynamic_update_slice_in_dim(out, value, index * rows, axis=dim)  17 us
    dot_general x1, matrix products, attend(): jnp.einsum('whqk,wkhd->wqhd', weights, kv_win[:, :, 1], preferred_element...  11.2 us
    dot_general x1, matrix products, per_device(): kv_sum = jnp.dot(scaled, projection, preferred_element_type=jnp.float32)  9.86 us
  transfers between devices with their start and end apart: 6, of which 3 were waited for; matrix products, arithmetic and copies ran while one was open for 34% of the time, Pallas kernels for 0%

profile of v1, /device:TPU:0, one launch (start us, length us, event | category | flops | bytes accessed | tf_op | source)
XLA Modules:
  0.0 278.0 jit_solution(6865820319755052955)
XLA Ops:
  4.3 7.3 %all-to-all-start = ((s32[8,1,4]{2,1,0:T(1,128)}), s32[8,1,4]{2,1,0:T(1,128)S(1)}, u32[]{:S(2)}, u32[]{:S(2)}) async-start(s32[8,1,4]{2,1,0:T(1,128)} %bitcast.2), calls=%async_computation | async-start | bytes 8192 | tf_op jit(solution)/shard_map/all_to_all | solution.py:69
  11.5 1.9 reshape.89
  13.4 4.5 %all-to-all-done = s32[8,1,4]{2,1,0:T(1,128)S(1)} async-done(((s32[8,1,4]{2,1,0:T(1,128)}), s32[8,1,4]{2,1,0:T(1,128)S(1)}, u32[]{:S(2)}, u32[]{:S(2)}) %all-to-all-start) | async-done | bytes 160 | tf_op jit(solution)/shard_map/all_to_all | solution.py:69
  22.4 2.5 pad_maximum_fusion.1
  24.9 3.8 %all-to-all-start.1 = ((bf16[8,4,2,14336]{3,1,2,0:T(4,128)(2,1)}), bf16[8,4,2,14336]{3,1,2,0:T(4,128)(2,1)S(1)}, u32[]{:S(2)}, u32[]{:S(2)}) async-start(bf16[8,4,2,14336]{3,1,2,0:T(4,128)(2,1)} %pad_maximum_fusion.1), calls=%async_computation.1 | async-start | bytes 3670016 | tf_op jit(solution)/shard_map/all_to_all | solution.py:77
  28.7 41.2 %all-to-all-done.1 = bf16[8,4,2,14336]{3,1,2,0:T(4,128)(2,1)S(1)} async-done(((bf16[8,4,2,14336]{3,1,2,0:T(4,128)(2,1)}), bf16[8,4,2,14336]{3,1,2,0:T(4,128)(2,1)S(1)}, u32[]{:S(2)}, u32[]{:S(2)}) %all-to-all-start.1) | async-done | bytes 1835040 | tf_op jit(solution)/shard_map/all_to_all | solution.py:77
  69.8 3.1 %copy.60 = bf16[8,4,2,14336]{3,2,1,0:T(2,128)(2,1)} copy(bf16[8,4,2,14336]{3,1,2,0:T(4,128)(2,1)S(1)} %all-to-all-done.1) | data formatting | bytes 3670016 | tf_op jit(solution)/shard_map/all_to_all | solution.py:77
  73.0 5.3 %gather_fusion = bf16[28,2,14336]{2,1,0:T(2,128)(2,1)S(1)} fusion(bf16[32,2,14336]{2,1,0:T(2,128)(2,1)} %bitcast.48, s32[1024]{0:T(1024)S(1)} %pad_clamp_fusion), kind=kCustom, calls=%fused_computation.2 | custom fusion | bytes 3211376 | tf_op jit(solution)/shard_map/jit(_take)/gather | solution.py:78
  78.3 1.5 broadcast_select_fusion
  79.8 2.4 select_n.62
  82.2 2.6 copy.61
  84.8 1.7 collective-permute-start.1
  86.5 34.0 %collective-permute-done = bf16[3584,224]{0,1:T(8,128)(2,1)S(1)} collective-permute-done((bf16[3584,224]{0,1:T(8,128)(2,1)}, bf16[3584,224]{0,1:T(8,128)(2,1)S(1)}, u32[]{:S(2)}, u32[]{:S(2)}) %collective-permute-start) | collective-permute-done | bytes 1605664 | tf_op jit(solution)/shard_map/ppermute | solution.py:20
  120.9 3.2 %copy.73 = bf16[112,8,2,512]{3,1,2,0:T(8,128)(2,1)} copy(bf16[112,8,2,512]{3,2,1,0:T(2,128)(2,1)} %bitcast.52) | data formatting | bytes 3670016
  124.1 3.2 %broadcast_in_dim.40 = bf16[3584,896]{1,0:T(8,128)(2,1)} broadcast(bf16[]{:T(256)} %constant.41.clone.1), dimensions={} | broadcast | bytes 6422530 | tf_op jit(solution)/shard_map/broadcast_in_dim | solution.py:15
  127.3 17.0 %dynamic_update_slice.12 = bf16[3584,896]{1,0:T(8,128)(2,1)} dynamic-update-slice(bf16[3584,896]{1,0:T(8,128)(2,1)} %broadcast_in_dim.40, bf16[3584,224]{1,0:T(8,128)(2,1)S(1)} %select_n.62, s32[]{:T(128)} %constant.49.clone.1, s32[]{:T(128)S(6)} %select_n.63) | dynamic-update-slice | bytes 3211268 | tf_op jit(solution)/shard_map/dynamic_update_slice | solution.py:16
  144.2 1.4 copy.62
  145.7 18.2 %dynamic_update_slice.13 = bf16[3584,896]{1,0:T(8,128)(2,1)} dynamic-update-slice(bf16[3584,896]{1,0:T(8,128)(2,1)} %dynamic_update_slice.12, bf16[3584,224]{1,0:T(8,128)(2,1)S(1)} %copy.62, s32[]{:T(128)} %constant.49.clone.1, s32[]{:T(128)S(6)} %select_n.65) | dynamic-update-slice | bytes 3211268 | tf_op jit(solution)/shard_map/dynamic_update_slice | solution.py:21
  163.9 2.8 %copy.64 = bf16[3584,224]{1,0:T(8,128)(2,1)S(1)} copy(bf16[3584,224]{0,1:T(8,128)(2,1)} %collective-permute-done.1) | data formatting | bytes 3211264 | tf_op jit(solution)/shard_map/ppermute | solution.py:23
  166.7 19.0 %dynamic_update_slice.14 = bf16[3584,896]{1,0:T(8,128)(2,1)} dynamic-update-slice(bf16[3584,896]{1,0:T(8,128)(2,1)} %dynamic_update_slice.13, bf16[3584,224]{1,0:T(8,128)(2,1)S(1)} %copy.64, s32[]{:T(128)} %constant.49.clone.1, s32[]{:T(128)S(6)} %select_n.67) | dynamic-update-slice | bytes 3211268 | tf_op jit(solution)/shard_map/dynamic_update_slice | solution.py:24
  185.8 2.8 %copy.65 = bf16[3584,224]{1,0:T(8,128)(2,1)S(1)} copy(bf16[3584,224]{0,1:T(8,128)(2,1)} %collective-permute-done.2) | data formatting | bytes 3211264 | tf_op jit(solution)/shard_map/ppermute | solution.py:20
  188.6 19.1 %dynamic_update_slice.15 = bf16[3584,896]{1,0:T(8,128)(2,1)} dynamic-update-slice(bf16[3584,896]{1,0:T(8,128)(2,1)} %dynamic_update_slice.14, bf16[3584,224]{1,0:T(8,128)(2,1)S(1)} %copy.65, s32[]{:T(128)} %constant.49.clone.1, s32[]{:T(128)S(6)} %select_n.69) | dynamic-update-slice | bytes 3211268 | tf_op jit(solution)/shard_map/dynamic_update_slice | solution.py:21
  207.7 4.3 %fusion.2 = f32[3584]{0:T(1024)S(1)} fusion(bf16[3584,896]{1,0:T(8,128)(2,1)} %dynamic_update_slice.15), kind=kLoop, calls=%fused_computation.9 | loop fusion | flops 9630208 | bytes 6436864 | tf_op jit(solution)/shard_map/reduce_sum | solution.py:83
  212.3 9.9 %multiply_convert_fusion = bf16[3584,1024]{0,1:T(8,128)(2,1)S(1)} fusion(bf16[896,1024]{1,0:T(8,128)(2,1)} %bitcast.53, f32[3584]{0:T(1024)S(1)} %add_rsqrt_fusion, bf16[3584,896]{1,0:T(8,128)(2,1)S(1)} %copy-done, f32[896]{0:T(1024)S(1)} %copy-done.4), kind=kOutput, calls=%fused_computation.7 | convolution fusion | flops 6593642496 | bytes 15615488 | tf_op jit(solution)/shard_map/dot_general | solution.py:82
  222.2 3.0 %copy-done.1 = bf16[3584,1024]{0,1:T(8,128)(2,1)} copy-done((bf16[3584,1024]{0,1:T(8,128)(2,1)}, bf16[3584,1024]{0,1:T(8,128)(2,1)S(1)}, u32[]{:S(2)}) %copy-start.1) | copy-done | bytes 7340056
  226.3 3.6 %collective-permute-start.3 = (bf16[256,2,4,128]{3,0,2,1:T(8,128)(2,1)}, bf16[256,2,4,128]{3,0,2,1:T(8,128)(2,1)S(1)}, u32[]{:S(2)}, u32[]{:S(2)}) collective-permute-start(bf16[256,2,4,128]{3,0,2,1:T(8,128)(2,1)} %copy.66), channel_id=1, source_target_pairs={{0,4},{4,8},{8,12},{12,16},{16,20},{20,24},{24,28},{1,5},{5,9},{9,... | collective-permute-start | bytes 1572872 | tf_op jit(solution)/shard_map/ppermute | solution.py:33
  230.6 13.4 %reshape.139 = bf16[14,256,2,4,128]{1,0,4,3,2:T(8,128)(2,1)} reshape(bf16[3584,1024]{0,1:T(8,128)(2,1)} %copy-done.1) | data formatting | bytes 14680064 | tf_op jit(solution)/shard_map/reshape | solution.py:86
  244.0 14.2 %copy.68 = bf16[14,256,2,4,128]{4,1,3,0,2:T(8,128)(2,1)} copy(bf16[14,256,2,4,128]{1,0,4,3,2:T(8,128)(2,1)} %reshape.139) | data formatting | bytes 14680064 | tf_op jit(solution)/shard_map/reshape | solution.py:86
  258.3 3.1 %fusion.7 = f32[15,4,64,256]{3,2,1,0:T(8,128)S(1)} fusion(bf16[1,256,2,4,128]{4,1,3,0,2:T(8,128)(2,1)S(1)} %bitcast.54, bf16[14,256,2,4,128]{4,1,3,0,2:T(8,128)(2,1)} %copy.68, bf16[15,64,4,128]{3,2,1,0:T(4,128)(2,1)S(1)} %reshape.93), kind=kOutput, calls=%fused_computation.15 | convolution fusion | flops 253624320 | bytes 12779520 | tf_op jit(solution)/shard_map/wqhd,wkhd->whqk/dot_general | solution.py:37
  261.4 1.9 copy-done.2
  263.3 1.5 fusion.39
  264.7 11.2 %fusion.21 = bf16[15,64,4,128]{3,1,2,0:T(8,128)(2,1)S(1)} fusion(bf16[14,256,2,4,128]{4,1,3,0,2:T(8,128)(2,1)} %copy.68, bf16[1,256,2,4,128]{4,1,3,0,2:T(8,128)(2,1)S(1)} %bitcast.55, f32[15,4,64]{2,1,0:T(4,128)S(1)} %fusion.39, f32[15,4,64,256]{3,2,1,0:T(8,128)} %copy-done.2), kind=kOutput, calls=%fused_computation.29 | convolution fusion | flops 264933376 | bytes 12794880 | tf_op jit(solution)/shard_map/whqk,wkhd->wqhd/dot_general | solution.py:43
  (56 shorter events, 13.3 us)
Async XLA Ops:
  4.3 13.6 %all-to-all-start = ((s32[8,1,4]{2,1,0:T(1,128)}), s32[8,1,4]{2,1,0:T(1,128)S(1)}, u32[]{:S(2)}, u32[]{:S(2)}) async-start(s32[8,1,4]{2,1,0:T(1,128)} %bitcast.2), calls=%async_computation | async-start | bytes 8192 | tf_op jit(solution)/shard_map/all_to_all | solution.py:69
  24.9 45.0 %all-to-all-start.1 = ((bf16[8,4,2,14336]{3,1,2,0:T(4,128)(2,1)}), bf16[8,4,2,14336]{3,1,2,0:T(4,128)(2,1)S(1)}, u32[]{:S(2)}, u32[]{:S(2)}) async-start(bf16[8,4,2,14336]{3,1,2,0:T(4,128)(2,1)} %pad_maximum_fusion.1), calls=%async_computation.1 | async-start | bytes 3670016 | tf_op jit(solution)/shard_map/all_to_all | solution.py:77
  84.8 35.7 %collective-permute-start = (bf16[3584,224]{0,1:T(8,128)(2,1)}, bf16[3584,224]{0,1:T(8,128)(2,1)S(1)}, u32[]{:S(2)}, u32[]{:S(2)}) collective-permute-start(bf16[3584,224]{0,1:T(8,128)(2,1)} %copy.61), channel_id=1, source_target_pairs={{0,1},{1,2},{2,3},{3,0},{4,5},{5,6},{6,7},{7,4},{8,9},{9,10},{10,1... | collective-permute-start | bytes 4816904 | tf_op jit(solution)/shard_map/ppermute | solution.py:20
  84.8 79.1 %collective-permute-start.1 = (bf16[3584,224]{0,1:T(8,128)(2,1)}, bf16[3584,224]{0,1:T(8,128)(2,1)}, u32[]{:S(2)}, u32[]{:S(2)}) collective-permute-start(bf16[3584,224]{0,1:T(8,128)(2,1)} %copy.61), channel_id=1, source_target_pairs={{0,3},{1,0},{2,1},{3,2},{4,7},{5,4},{6,5},{7,6},{8,11},{9,8},{10,9... | collective-permute-start | bytes 4816904 | tf_op jit(solution)/shard_map/ppermute | solution.py:23
  120.5 65.3 %collective-permute-start.2 = (bf16[3584,224]{0,1:T(8,128)(2,1)S(1)}, bf16[3584,224]{0,1:T(8,128)(2,1)}, u32[]{:S(2)}, u32[]{:S(2)}) collective-permute-start(bf16[3584,224]{0,1:T(8,128)(2,1)S(1)} %collective-permute-done), channel_id=1, source_target_pairs={{0,1},{1,2},{2,3},{3,0},{4,5},{5,6},{6,7},{7,4},{8,9},{9,10},{10,1... | collective-permute-start | bytes 4816904 | tf_op jit(solution)/shard_map/ppermute | solution.py:20
  207.7 4.7 %copy-start = (bf16[3584,896]{1,0:T(8,128)(2,1)S(1)}, bf16[3584,896]{1,0:T(8,128)(2,1)}, u32[]{:S(2)}) copy-start(bf16[3584,896]{1,0:T(8,128)(2,1)} %dynamic_update_slice.15) | copy-start | bytes 19267588
  207.7 4.7 %copy-start.4 = (f32[896]{0:T(1024)S(1)}, f32[896]{0:T(1024)}, u32[]{:S(2)}) copy-start(f32[896]{0:T(1024)} %param.10) | copy-start | bytes 10756
  212.3 17.6 %copy-start.3 = (bf16[896,512]{1,0:T(8,128)(2,1)S(1)}, bf16[896,512]{1,0:T(8,128)(2,1)}, u32[]{:S(2)}) copy-start(bf16[896,512]{1,0:T(8,128)(2,1)} %param.8) | copy-start | bytes 2752516
  222.2 3.0 %copy-start.1 = (bf16[3584,1024]{0,1:T(8,128)(2,1)}, bf16[3584,1024]{0,1:T(8,128)(2,1)S(1)}, u32[]{:S(2)}) copy-start(bf16[3584,1024]{0,1:T(8,128)(2,1)S(1)} %multiply_convert_fusion) | copy-start | bytes 22020100
  226.3 32.0 %collective-permute-start.3 = (bf16[256,2,4,128]{3,0,2,1:T(8,128)(2,1)}, bf16[256,2,4,128]{3,0,2,1:T(8,128)(2,1)S(1)}, u32[]{:S(2)}, u32[]{:S(2)}) collective-permute-start(bf16[256,2,4,128]{3,0,2,1:T(8,128)(2,1)} %copy.66), channel_id=1, source_target_pairs={{0,4},{4,8},{8,12},{12,16},{16,20},{20,24},{24,28},{1,5},{5,9},{9,... | collective-permute-start | bytes 1572872 | tf_op jit(solution)/shard_map/ppermute | solution.py:33
  261.4 1.9 copy-start.2
